TPU v7x, 256 devices: a whole 4x4x8 slice. The times are simulated.
256 devices in a mesh: dp: 4 (over x), frame: 32 (over z, y), spatial: 2 (over core).
Axes of the slice: x: 4, y: 4, z: 8, core: 2. Of those that a mesh axis runs over, the one named last changes fastest.
Arguments:
- queries: bfloat16 [4, 32, 256, 3072], P('dp', 'frame', 'spatial'), may hold values from -120 to 120
- key_states: bfloat16 [4, 32, 256, 3072], P('dp', 'frame', 'spatial'), may hold values from -6 to 6
- value_states: bfloat16 [4, 32, 256, 3072], P('dp', 'frame', 'spatial'), may hold values from -6 to 6
- out_grad: bfloat16 [4, 32, 256, 3072], P('dp', 'frame', 'spatial'), may hold values from -6 to 6
- head_slopes: float32 [24], replicated, may hold values from 0.05 to 2
- timesteps: int32 [4, 32], P('dp', 'frame'), may hold values from 0 to 999
- stretch_frames: int32 [4, 32], P('dp', 'frame'), may hold values from 3 to 96, as said below
- valid_counts: int32 [4, 32], P('dp', 'frame'), may hold values from 64 to 256, as said below
- mod_weight: float32 [256, 3072], replicated, may hold values from -0.375 to 0.375
Outputs:
- query_grad: bfloat16 [4, 32, 256, 3072], P('dp', 'frame', 'spatial')
- key_grad: bfloat16 [4, 32, 256, 3072], P('dp', 'frame', 'spatial')
- value_grad: bfloat16 [4, 32, 256, 3072], P('dp', 'frame', 'spatial')
- mod_weight_grad: float32 [256, 3072], replicated
Inputs may be any that keep to these rules, and one draw needn't show every extreme that they name: `stretch_frames`: strictly increasing along each video's stretches, by 1 to 3 frames a stretch; each video's last stretch stands at frame 3 * 32. `valid_counts`: in every video some stretch is full.
All inputs are finite; a program needn't handle non-finite values.
Results may differ from a plain program's by a relative error of at most 0.02.
Values may be sent and summed in bfloat16 or wider, within the bound.
A program may use at most 128 MiB of HBM per device.

v0:
```python
import math

import jax
import jax.numpy as jnp
from jax import lax
from jax.sharding import PartitionSpec as P

FREQ = 256
SPAN = 3


def shifted(block, axis, distance):
    devices = range(lax.axis_size(axis))
    route = [(i - distance, i) for i in devices if i - distance in devices]
    return lax.ppermute(block, axis, route)


def timestep_embedding(steps):
    half_count = FREQ // 2
    frequencies = jnp.exp(
        -math.log(10000.0) * jnp.arange(half_count, dtype=jnp.float32) / half_count
    )
    angles = steps.astype(jnp.float32)[..., None] * frequencies
    return jnp.concatenate([jnp.cos(angles), jnp.sin(angles)], axis=-1)


def local(
    queries,
    key_states,
    value_states,
    out_grad,
    head_slopes,
    timesteps,
    stretch_frames,
    valid_counts,
    mod_weight,
):
    tok_rows = queries.shape[2]
    full_width = queries.shape[3]
    head_count = head_slopes.shape[0]
    head_size = full_width // head_count
    spatial_size = lax.axis_size("spatial")
    local_heads = head_count // spatial_size
    channels = local_heads * head_size
    score_scale = head_size ** (-0.5)

    def by_heads(values):
        return values.reshape(tok_rows, head_count, head_size)

    query_local, keys_own, values_own, grad_own = (
        lax.all_to_all(by_heads(queries), "spatial", split_axis=1, concat_axis=0, tiled=True),
        lax.all_to_all(by_heads(key_states), "spatial", split_axis=1, concat_axis=0, tiled=True),
        lax.all_to_all(by_heads(value_states), "spatial", split_axis=1, concat_axis=0, tiled=True),
        lax.all_to_all(by_heads(out_grad), "spatial", split_axis=1, concat_axis=0, tiled=True),
    )
    tokens = query_local.shape[0]
    head_group = lax.axis_index("spatial")
    slopes = lax.dynamic_slice_in_dim(head_slopes, head_group * local_heads, local_heads, 0)
    weight_half = lax.dynamic_slice_in_dim(mod_weight, head_group * channels, channels, 1)
    embedding = timestep_embedding(timesteps[0, 0])
    gate_vec = jnp.dot(embedding[None, :], weight_half, precision=lax.Precision.HIGHEST).reshape(
        local_heads, head_size
    )
    count_now = valid_counts[0, 0]
    frame_now = stretch_frames[0, 0]
    key_list = [keys_own]
    value_list = [values_own]
    count_list = [valid_counts.reshape(1)]
    frame_list = [stretch_frames.reshape(1)]
    for distance in range(1, SPAN + 1):
        arrived = shifted((keys_own, values_own, valid_counts, stretch_frames), "frame", distance)
        key_list.append(arrived[0])
        value_list.append(arrived[1])
        count_list.append(arrived[2].reshape(1))
        frame_list.append(arrived[3].reshape(1))
    key_window = jnp.stack(key_list)
    value_window = jnp.stack(value_list)
    count_window = jnp.concatenate(count_list)
    frame_window = jnp.concatenate(frame_list)
    key_flat = key_window.reshape(-1, local_heads, head_size)
    value_flat = value_window.reshape(-1, local_heads, head_size)
    distance_keys = jnp.repeat((frame_now - frame_window).astype(jnp.float32), tokens)
    visible = (jnp.arange(tokens, dtype=jnp.int32)[None, :] < count_window[:, None]).reshape(-1)
    scores = (
        jnp.einsum("ihe,jhe->hij", query_local, key_flat, preferred_element_type=jnp.float32)
        * score_scale
    )
    scores = scores - slopes[:, None, None] * distance_keys[None, None, :]
    scores = jnp.where(visible[None, None, :], scores, -jnp.inf)
    row_max = jnp.max(scores, axis=2)
    exp_scores = jnp.exp(scores - row_max[:, :, None])
    inv_sum = 1.0 / jnp.sum(exp_scores, axis=2)
    attn_prob = exp_scores * inv_sum[:, :, None]
    attn_low = attn_prob.astype(jnp.bfloat16)
    attended = jnp.einsum("hij,jhe->ihe", attn_low, value_flat, preferred_element_type=jnp.float32)
    live_rows = (jnp.arange(tokens, dtype=jnp.int32) < count_now).astype(jnp.float32)[:, None, None]
    grad_float = grad_own.astype(jnp.float32)
    gated_grad = (gate_vec[None] * grad_float * live_rows).astype(jnp.bfloat16)
    gate_grad = jnp.sum(grad_float * attended * live_rows, axis=0).reshape(-1)
    row_delta = jnp.einsum("ihe,ihe->hi", gated_grad.astype(jnp.float32), attended)
    grad_prob = jnp.einsum(
        "ihe,jhe->hij", gated_grad, value_flat, preferred_element_type=jnp.float32
    )
    grad_score = (attn_prob * (grad_prob - row_delta[:, :, None]) * score_scale).astype(
        jnp.bfloat16
    )
    query_grad = jnp.einsum(
        "hij,jhe->ihe", grad_score, key_flat, preferred_element_type=jnp.float32
    ).astype(jnp.bfloat16)
    key_parts = jnp.einsum(
        "hij,ihe->jhe", grad_score, query_local, preferred_element_type=jnp.float32
    ).reshape(SPAN + 1, tokens, local_heads, head_size)
    value_parts = jnp.einsum(
        "hij,ihe->jhe", attn_low, gated_grad, preferred_element_type=jnp.float32
    ).reshape(SPAN + 1, tokens, local_heads, head_size)
    key_total = key_parts[0]
    value_total = value_parts[0]
    for distance in range(1, SPAN + 1):
        arrived = (
            shifted(key_parts[distance].astype(jnp.bfloat16), "frame", -distance).astype(
                jnp.float32
            ),
            shifted(value_parts[distance].astype(jnp.bfloat16), "frame", -distance).astype(
                jnp.float32
            ),
        )
        key_total = key_total + arrived[0]
        value_total = value_total + arrived[1]
    query_back, key_back, value_back = (
        lax.all_to_all(query_grad, "spatial", split_axis=0, concat_axis=1, tiled=True),
        lax.all_to_all(
            key_total.astype(jnp.bfloat16), "spatial", split_axis=0, concat_axis=1, tiled=True
        ),
        lax.all_to_all(
            value_total.astype(jnp.bfloat16), "spatial", split_axis=0, concat_axis=1, tiled=True
        ),
    )
    out_shape = (1, 1, tok_rows, full_width)
    weight_block = lax.psum(embedding[:, None] * gate_grad[None, :], ("dp", "frame"))
    mod_weight_grad = lax.all_gather(
        weight_block.astype(jnp.bfloat16), "spatial", axis=1, tiled=True
    ).astype(weight_block.dtype)
    return (
        query_back.reshape(out_shape),
        key_back.reshape(out_shape),
        value_back.reshape(out_shape),
        mod_weight_grad,
    )


def solution(mesh):
    in_specs = (
        P("dp", "frame", "spatial", None),
        P("dp", "frame", "spatial", None),
        P("dp", "frame", "spatial", None),
        P("dp", "frame", "spatial", None),
        P(),
        P("dp", "frame"),
        P("dp", "frame"),
        P("dp", "frame"),
        P(),
    )
    out_specs = (
        P("dp", "frame", "spatial", None),
        P("dp", "frame", "spatial", None),
        P("dp", "frame", "spatial", None),
        P(),
    )
    return jax.shard_map(local, mesh=mesh, in_specs=in_specs, out_specs=out_specs, check_vma=False)
```

profile of v0, /device:TPU:1, one launch (start us, length us, event | category | flops | bytes accessed | tf_op | source)
XLA Modules:
  0.0 960.6 jit_solution(2260432892829903640)
XLA Ops:
  9.6 9.2 all_to_all.108
  21.1 3.8 collective-permute-start.2
  24.9 4.5 collective-permute-start.1
  32.1 4.0 collective-permute-start.8
  36.0 3.9 collective-permute-start.7
  42.2 6.1 all-to-all-start.1
  51.9 4.3 all-to-all-start.3
  66.1 3.5 all-to-all-start.2
  75.4 5.3 collective-permute-start.5
  80.8 6.2 collective-permute-start.4
  90.9 5.9 collective-permute-start.11
  99.2 2.9 collective-permute-start.9
  108.2 19.8 %collective-permute-done.11 = bf16[256,12,128]{2,0,1:T(8,128)(2,1)} collective-permute-done((bf16[256,12,128]{2,0,1:T(8,128)(2,1)}, bf16[256,12,128]{2,0,1:T(8,128)(2,1)}, u32[]{:S(2)}, u32[]{:S(2)}) %collective-permute-start.11) | collective-permute-done | bytes 786464 | tf_op jit(solution)/shard_map/ppermute | solution.py:15
  132.2 8.7 fusion.32
  140.9 8.0 fusion.20
  150.3 5.2 multiply_convert_fusion
  155.6 7.3 fusion.33
  166.3 609.0 %all-reduce.1 = bf16[256,1536]{1,0:T(8,128)(2,1)} all-reduce(f32[256,1536]{1,0:T(8,128)S(1)} %broadcast_multiply_fusion), channel_id=1, replica_groups=mesh['dp'=4,'frame'=32,'spatial'=2] {'dp','frame'}, use_global_device_ids=true, to_apply=%region_3.4 | all-reduce | flops 393216 | bytes 2359296 | tf_op jit(solution)/shard_map/psum | solution.py:139
  775.4 9.4 fusion.34
  793.3 4.9 fusion.21
  800.0 124.0 %all_to_all.109 = bf16[256,12,128]{2,1,0:T(8,128)(2,1)S(1)} all-to-all(bf16[256,12,128]{2,1,0:T(8,128)(2,1)S(1)} %copy.132), channel_id=1, replica_groups=mesh['dp'=4,'frame'=32,'spatial'=2] {'spatial'}, dimensions={0} | all-to-all | bytes 1572864 | tf_op jit(solution)/shard_map/all_to_all | solution.py:130
  929.0 7.2 all_to_all.110
  941.8 4.6 all_to_all.111
  950.3 3.4 convert_element_type.102
  (92 shorter events, 73.0 us)
Async XLA Ops:
  7.2 54.3 %copy-start = (f32[256,3072]{1,0:T(8,128)S(1)}, f32[256,3072]{1,0:T(8,128)}, u32[]{:S(2)}) copy-start(f32[256,3072]{1,0:T(8,128)} %param.17) | copy-start | bytes 9437188
  21.1 78.1 %collective-permute-start.2 = (bf16[256,12,128]{2,0,1:T(8,128)(2,1)}, bf16[256,12,128]{2,0,1:T(8,128)(2,1)}, u32[]{:S(2)}, u32[]{:S(2)}) collective-permute-start(bf16[256,12,128]{2,0,1:T(8,128)(2,1)} %bitcast.136), channel_id=1, source_target_pairs={{0,6},{2,8},{4,10},{6,12},{8,14},{10,16},{12,18},{14,20},{16,22},{... | collective-permute-start | bytes 2359304 | tf_op jit(solution)/shard_map/ppermute | solution.py:15
  24.9 79.2 %collective-permute-start.1 = (bf16[256,12,128]{2,0,1:T(8,128)(2,1)}, bf16[256,12,128]{2,0,1:T(8,128)(2,1)}, u32[]{:S(2)}, u32[]{:S(2)}) collective-permute-start(bf16[256,12,128]{2,0,1:T(8,128)(2,1)} %bitcast.137), channel_id=1, source_target_pairs={{0,4},{2,6},{4,8},{6,10},{8,12},{10,14},{12,16},{14,18},{16,20},{1... | collective-permute-start | bytes 2359304 | tf_op jit(solution)/shard_map/ppermute | solution.py:15
  29.4 74.7 %collective-permute-start = (bf16[256,12,128]{2,0,1:T(8,128)(2,1)}, bf16[256,12,128]{2,0,1:T(8,128)(2,1)}, u32[]{:S(2)}, u32[]{:S(2)}) collective-permute-start(bf16[256,12,128]{2,0,1:T(8,128)(2,1)} %bitcast.138), channel_id=1, source_target_pairs={{0,2},{2,4},{4,6},{6,8},{8,10},{10,12},{12,14},{14,16},{16,18},{18... | collective-permute-start | bytes 2359304 | tf_op jit(solution)/shard_map/ppermute | solution.py:15
  32.1 41.4 %collective-permute-start.8 = (s32[1,1]{1,0:T(1,128)}, s32[1,1]{1,0:T(1,128)}, u32[]{:S(2)}, u32[]{:S(2)}) collective-permute-start(s32[1,1]{1,0:T(1,128)} %param.15), channel_id=1, source_target_pairs={{0,6},{2,8},{4,10},{6,12},{8,14},{10,16},{12,18},{14,20},{16,22},{... | collective-permute-start | bytes 20 | tf_op jit(solution)/shard_map/ppermute | solution.py:15
  36.0 39.4 %collective-permute-start.7 = (s32[1,1]{1,0:T(1,128)}, s32[1,1]{1,0:T(1,128)}, u32[]{:S(2)}, u32[]{:S(2)}) collective-permute-start(s32[1,1]{1,0:T(1,128)} %param.15), channel_id=1, source_target_pairs={{0,4},{2,6},{4,8},{6,10},{8,12},{10,14},{12,16},{14,18},{16,20},{1... | collective-permute-start | bytes 20 | tf_op jit(solution)/shard_map/ppermute | solution.py:15
  42.2 9.7 %all-to-all-start.1 = ((bf16[128,24,128]{0,2,1:T(8,128)(2,1)}), bf16[128,24,128]{0,2,1:T(8,128)(2,1)}, u32[]{:S(2)}, u32[]{:S(2)}) async-start(bf16[128,24,128]{0,2,1:T(8,128)(2,1)} %bitcast.144), calls=%async_computation.1 | async-start | bytes 1572864 | tf_op jit(solution)/shard_map/all_to_all | solution.py:51
  51.9 14.2 %all-to-all-start.3 = ((bf16[128,24,128]{0,2,1:T(8,128)(2,1)}), bf16[128,24,128]{0,2,1:T(8,128)(2,1)}, u32[]{:S(2)}, u32[]{:S(2)}) async-start(bf16[128,24,128]{0,2,1:T(8,128)(2,1)} %bitcast.143), calls=%async_computation.3 | async-start | bytes 1572864 | tf_op jit(solution)/shard_map/all_to_all | solution.py:53
  66.1 6.0 all-to-all-start.2
  69.7 880.6 %all-gather.2.cloned.1.call-start = ((), (), s32[]{:S(2)}) async-start(), calls=%async_computation.7 | async-start | bytes 2359296 | tf_op jit(solution)/shard_map/all_gather | solution.py:140
  73.4 7.3 collective-permute-start.6
  75.4 13.6 %collective-permute-start.5 = (s32[1,1]{1,0:T(1,128)}, s32[1,1]{1,0:T(1,128)}, u32[]{:S(2)}, u32[]{:S(2)}) collective-permute-start(s32[1,1]{1,0:T(1,128)} %param.16), channel_id=1, source_target_pairs={{0,6},{2,8},{4,10},{6,12},{8,14},{10,16},{12,18},{14,20},{16,22},{... | collective-permute-start | bytes 20 | tf_op jit(solution)/shard_map/ppermute | solution.py:15
  80.8 10.1 %collective-permute-start.4 = (s32[1,1]{1,0:T(1,128)}, s32[1,1]{1,0:T(1,128)}, u32[]{:S(2)}, u32[]{:S(2)}) collective-permute-start(s32[1,1]{1,0:T(1,128)} %param.16), channel_id=1, source_target_pairs={{0,4},{2,6},{4,8},{6,10},{8,12},{10,14},{12,16},{14,18},{16,20},{1... | collective-permute-start | bytes 20 | tf_op jit(solution)/shard_map/ppermute | solution.py:15
  89.0 7.8 collective-permute-start.3
  90.9 37.2 %collective-permute-start.11 = (bf16[256,12,128]{2,0,1:T(8,128)(2,1)}, bf16[256,12,128]{2,0,1:T(8,128)(2,1)}, u32[]{:S(2)}, u32[]{:S(2)}) collective-permute-start(bf16[256,12,128]{2,0,1:T(8,128)(2,1)} %bitcast.46), channel_id=1, source_target_pairs={{0,6},{2,8},{4,10},{6,12},{8,14},{10,16},{12,18},{14,20},{16,22},{... | collective-permute-start | bytes 2359304 | tf_op jit(solution)/shard_map/ppermute | solution.py:15
  96.8 31.2 %collective-permute-start.10 = (bf16[256,12,128]{2,0,1:T(8,128)(2,1)}, bf16[256,12,128]{2,0,1:T(8,128)(2,1)}, u32[]{:S(2)}, u32[]{:S(2)}) collective-permute-start(bf16[256,12,128]{2,0,1:T(8,128)(2,1)} %bitcast.46), channel_id=1, source_target_pairs={{0,4},{2,6},{4,8},{6,10},{8,12},{10,14},{12,16},{14,18},{16,20},{1... | collective-permute-start | bytes 2359304 | tf_op jit(solution)/shard_map/ppermute | solution.py:15
  99.2 30.6 %collective-permute-start.9 = (bf16[256,12,128]{2,0,1:T(8,128)(2,1)}, bf16[256,12,128]{2,0,1:T(8,128)(2,1)}, u32[]{:S(2)}, u32[]{:S(2)}) collective-permute-start(bf16[256,12,128]{2,0,1:T(8,128)(2,1)} %bitcast.46), channel_id=1, source_target_pairs={{0,2},{2,4},{4,6},{6,8},{8,10},{10,12},{12,14},{14,16},{16,18},{18... | collective-permute-start | bytes 2359304 | tf_op jit(solution)/shard_map/ppermute | solution.py:15
  164.4 627.3 %collective-permute-start.14 = (bf16[256,12,128]{2,0,1:T(8,128)(2,1)}, bf16[256,12,128]{2,0,1:T(8,128)(2,1)}, u32[]{:S(2)}, u32[]{:S(2)}) collective-permute-start(bf16[256,12,128]{2,0,1:T(8,128)(2,1)} %get-tuple-element.26), channel_id=1, source_target_pairs={{6,0},{8,2},{10,4},{12,6},{14,8},{16,10},{18,12},{20,14},{22,16},{... | collective-permute-start | bytes 2359304 | tf_op jit(solution)/shard_map/ppermute | solution.py:15
  166.1 609.2 %copy-start.5 = (bf16[256,12,128]{0,2,1:T(8,128)(2,1)S(1)}, bf16[256,12,128]{0,2,1:T(8,128)(2,1)}, u32[]{:S(2)}) copy-start(bf16[256,12,128]{0,2,1:T(8,128)(2,1)} %get-tuple-element.21) | copy-start | bytes 2359300
  784.8 141.2 %collective-permute-start.13 = (bf16[256,12,128]{2,0,1:T(8,128)(2,1)}, bf16[256,12,128]{2,0,1:T(8,128)(2,1)}, u32[]{:S(2)}, u32[]{:S(2)}) collective-permute-start(bf16[256,12,128]{2,0,1:T(8,128)(2,1)} %get-tuple-element.27), channel_id=1, source_target_pairs={{4,0},{6,2},{8,4},{10,6},{12,8},{14,10},{16,12},{18,14},{20,16},{2... | collective-permute-start | bytes 2359304 | tf_op jit(solution)/shard_map/ppermute | solution.py:15
  786.3 139.7 %collective-permute-start.12 = (bf16[256,12,128]{2,0,1:T(8,128)(2,1)}, bf16[256,12,128]{2,0,1:T(8,128)(2,1)}, u32[]{:S(2)}, u32[]{:S(2)}) collective-permute-start(bf16[256,12,128]{2,0,1:T(8,128)(2,1)} %get-tuple-element.25), channel_id=1, source_target_pairs={{2,0},{4,2},{6,4},{8,6},{10,8},{12,10},{14,12},{16,14},{18,16},{20... | collective-permute-start | bytes 2359304 | tf_op jit(solution)/shard_map/ppermute | solution.py:15
  789.1 149.1 %collective-permute-start.17 = (bf16[256,12,128]{0,2,1:T(8,128)(2,1)}, bf16[256,12,128]{0,2,1:T(8,128)(2,1)}, u32[]{:S(2)}, u32[]{:S(2)}) collective-permute-start(bf16[256,12,128]{0,2,1:T(8,128)(2,1)} %get-tuple-element.23), channel_id=1, source_target_pairs={{6,0},{8,2},{10,4},{12,6},{14,8},{16,10},{18,12},{20,14},{22,16},{... | collective-permute-start | bytes 2359304 | tf_op jit(solution)/shard_map/ppermute | solution.py:15
  790.4 147.8 %collective-permute-start.16 = (bf16[256,12,128]{0,2,1:T(8,128)(2,1)}, bf16[256,12,128]{0,2,1:T(8,128)(2,1)}, u32[]{:S(2)}, u32[]{:S(2)}) collective-permute-start(bf16[256,12,128]{0,2,1:T(8,128)(2,1)} %get-tuple-element.24), channel_id=1, source_target_pairs={{4,0},{6,2},{8,4},{10,6},{12,8},{14,10},{16,12},{18,14},{20,16},{2... | collective-permute-start | bytes 2359304 | tf_op jit(solution)/shard_map/ppermute | solution.py:15
  791.7 146.5 %collective-permute-start.15 = (bf16[256,12,128]{0,2,1:T(8,128)(2,1)}, bf16[256,12,128]{0,2,1:T(8,128)(2,1)}, u32[]{:S(2)}, u32[]{:S(2)}) collective-permute-start(bf16[256,12,128]{0,2,1:T(8,128)(2,1)} %get-tuple-element.22), channel_id=1, source_target_pairs={{2,0},{4,2},{6,4},{8,6},{10,8},{12,10},{14,12},{16,14},{18,16},{20... | collective-permute-start | bytes 2359304 | tf_op jit(solution)/shard_map/ppermute | solution.py:15
  (6 other events, 37.0 us)
Sparse Core Ops, SparseCore 0:
  775.5 126.8 all-gather.1
where the time goes:
time: 971 us; the launch traced here: 961 us
  blocking collectives  754 us (78%)
  starting transfers between devices  67.7 us (7%)
  matrix products  45 us (5%)
  local copies, waits for them, and re-layouts  37.7 us (4%)
  waiting for transfers between devices  21.6 us (2%)
  other arithmetic  18.3 us (2%)
  between operations  16.3 us (2%)
    psum x1, blocking collectives, local(): lax.psum(embedding[:, None] * gate_grad[None, :], ('dp', 'frame'))  609 us
    all_to_all x1, blocking collectives, local(): lax.all_to_all(query_grad, 'spatial', split_axis=0, concat_axis=1, tiled=...  124 us
    ppermute x18, starting transfers between devices, shifted(): return lax.ppermute(block, axis, route)  53.7 us
    ppermute x18, waiting for transfers between devices, shifted(): return lax.ppermute(block, axis, route)  21.6 us
  transfers between devices with their start and end apart: 22, of which 2 were waited for; matrix products, arithmetic and copies ran while one was open for 6% of the time, Pallas kernels for 0%

commit v1 on v0

v1 whole, which is shorter than its diff:
```python
import math

import jax
import jax.numpy as jnp
import numpy as np
from jax import lax
from jax.experimental import pallas as pl
from jax.experimental.pallas import tpu as pltpu
from jax.sharding import PartitionSpec as P

MESH = pl.DeviceIdType.MESH
F32 = jnp.float32
BF16 = jnp.bfloat16
HIGHEST = lax.Precision.HIGHEST

NX, NZ, NY, NS = 4, 8, 4, 2
GROUP = NY * NS
SPAN = 3
SLOTS = SPAN + NY
TOK = 256
PART = TOK // NS
HEAD = 128
HEADS = 24
MINE = HEADS // GROUP
CHUNK = MINE * HEAD
WIDTH = HEADS * HEAD
FREQ = 256
SCALE = HEAD ** (-0.5)
LOG2E = math.log2(math.e)
HIDDEN = -1e30
NT = (((1,), (1,)), ((), ()))
TN = (((0,), (0,)), ((), ()))


def dot(a, b, dims=(((1,), (0,)), ((), ()))):
    return lax.dot_general(a, b, dims, preferred_element_type=F32)


def main_kernel(
    freq_ref, slope_ref, step_ref, frame_ref, count_ref, weight_ref,
    q_in, k_in, v_in, g_in,
    dq_out, dk_out, dv_out, mod_out,
    qb, kb, vb, gb, kt, vt, weight, meta, times, rows_t, gate, emb_hi, emb_lo, bias,
    x_s, p_s, d_s, dk_acc, dv_acc, dq_s, dk_s, dv_s, halo_s, halo_r, dgate, terms,
    in_recv, in_send, z_recv, z_send, h_recv, h_send, o_recv, o_send, o_loc,
    m_recv, m_send, t_recv, t_send, w_sem,
):
    x = lax.axis_index("dp")
    frame = lax.axis_index("frame")
    s = lax.axis_index("spatial")
    z = frame // NY
    y = frame % NY
    p = y * NS + s

    def group_dev(k):
        other = (p + k) % GROUP
        return (x, z * NY + other // NS, other % NS), other

    def y_dev(k):
        return (x, z * NY + (y + k) % NY, s)

    def z_dev(k):
        return (x, ((z + k) % NZ) * NY + y, s)

    def x_dev(k):
        return ((x + k) % NX, frame, s)

    def loop(low, high, body):
        def step(k, carry):
            body(k)
            return carry

        lax.fori_loop(low, high, step, 0)

    def send(src, dst, send_sem, recv_sem, device):
        pltpu.make_async_remote_copy(
            src_ref=src, dst_ref=dst, send_sem=send_sem, recv_sem=recv_sem,
            device_id=device, device_id_type=MESH,
        ).start()

    def wait(ref, sem):
        pltpu.make_async_copy(ref, ref, sem).wait()

    barrier = pltpu.get_barrier_semaphore()

    def greet(device):
        pl.semaphore_signal(barrier, inc=1, device_id=device, device_id_type=MESH)

    loop(1, GROUP, lambda k: greet(group_dev(k)[0]))
    loop(1, NZ, lambda k: greet(z_dev(k)))
    loop(1, NX, lambda k: greet(x_dev(k)))

    weight_copy = pltpu.make_async_copy(
        weight_ref.at[:, pl.ds(pl.multiple_of(p * CHUNK, HEAD), CHUNK)], weight, w_sem
    )
    weight_copy.start()
    line = lax.broadcasted_iota(jnp.int32, (8, HEAD), 0)
    meta[y] = jnp.where(
        line == 0, count_ref[0], jnp.where(line == 1, frame_ref[0], step_ref[0])
    )
    arrays = ((k_in, kb, SPAN), (v_in, vb, SPAN), (q_in, qb, 0), (g_in, gb, 0))

    def column(owner, h):
        return pl.ds(pl.multiple_of(owner * CHUNK + h * HEAD, HEAD), HEAD)

    def own_part(a, h):
        src, dst, first = arrays[a]
        pltpu.make_async_copy(
            src.at[:, column(p, h)], dst.at[h, first + y, pl.ds(s * PART, PART)], in_recv.at[a, h]
        ).start()

    for a in range(4):
        loop(0, MINE, lambda h, a=a: own_part(a, h))

    pl.semaphore_wait(barrier, GROUP - 1 + NZ - 1 + NX - 1)

    loop(1, NY, lambda k: send(meta.at[y], meta.at[y], m_send.at[0], m_recv.at[0], y_dev(k)))

    def send_part(a, h, k):
        src, dst, first = arrays[a]
        device, owner = group_dev(k)
        send(
            src.at[:, column(owner, h)], dst.at[h, first + y, pl.ds(s * PART, PART)],
            in_send.at[a, h], in_recv.at[a, h], device,
        )

    def send_pair(first, h):
        for a in (first, first + 1):
            loop(1, GROUP, lambda k, a=a: send_part(a, h, k))

    loop(0, MINE, lambda h: send_pair(0, h))
    loop(0, MINE, lambda h: send_pair(2, h))

    wait(meta.at[pl.ds(0, NY - 1)], m_recv.at[0])
    times[x, z] = meta[...]
    loop(1, NZ, lambda k: send(meta, times.at[x, z], m_send.at[1], m_recv.at[1], z_dev(k)))
    rows_t[...] = jnp.zeros_like(rows_t)
    for i in range(NY):
        rows_t[i : i + 1, :] = meta[i, 2:3, :].astype(F32)
    angles = rows_t[0:8, :] * freq_ref[...]
    emb = jnp.concatenate([jnp.cos(angles), jnp.sin(angles)], axis=1)
    weight_copy.wait()
    gates = lax.dot_general(
        emb, weight[...], (((1,), (0,)), ((), ())), precision=HIGHEST, preferred_element_type=F32
    )
    for h in range(MINE):
        gate[h] = gates[:, h * HEAD : (h + 1) * HEAD]

    def pass_on(h):
        wait(kb.at[h, pl.ds(SPAN, NY)], in_recv.at[0, h])
        send(
            kb.at[h, pl.ds(NY, SPAN)], kb.at[h, pl.ds(0, SPAN)],
            z_send.at[0, h], z_recv.at[0, h], z_dev(1),
        )
        wait(vb.at[h, pl.ds(SPAN, NY)], in_recv.at[1, h])
        send(
            vb.at[h, pl.ds(NY, SPAN)], vb.at[h, pl.ds(0, SPAN)],
            z_send.at[1, h], z_recv.at[1, h], z_dev(1),
        )

    loop(0, 1, pass_on)
    wait(times.at[0, pl.ds(0, NZ - 1)], m_recv.at[1])
    loop(1, NX, lambda k: send(times.at[x], times.at[x], m_send.at[2], m_recv.at[2], x_dev(k)))
    loop(1, MINE, pass_on)

    wait(times.at[pl.ds(0, NX - 1)], m_recv.at[2])

    def take_row(n):
        for i in range(NY):
            rows_t[pl.ds(n * NY + i, 1), :] = times[n // NZ, n % NZ, i, 2:3, :].astype(F32)

    loop(0, NX * NZ, take_row)

    def features(n):
        angle = rows_t[pl.ds(pl.multiple_of(n * 8, 8), 8), :] * freq_ref[...]
        both = jnp.concatenate([jnp.cos(angle), jnp.sin(angle)], axis=1)
        for half in range(2):
            four = both[half * NY : (half + 1) * NY]
            tile = jnp.concatenate([four, four, four, four], axis=0)
            high = tile.astype(BF16)
            at = pl.ds(pl.multiple_of(n * 32 + half * 16, 16), 16)
            emb_hi[at, :] = high
            emb_lo[at, :] = (tile - high.astype(F32)).astype(BF16)

    loop(0, NX * NZ // 2, features)

    token = lax.broadcasted_iota(jnp.int32, (TOK, HEAD), 0)
    z_before = (z + NZ - 1) % NZ
    has_before = jnp.minimum(z, 1)
    base = times[x, z, NY - 1, 1:2, :]

    def head(h):
        wait(kb.at[h, pl.ds(0, SPAN)], z_recv.at[0, h])
        wait(vb.at[h, pl.ds(0, SPAN)], z_recv.at[1, h])
        kt[...] = kb[h].reshape(SLOTS * TOK, HEAD).T
        vt[...] = vb[h].reshape(SLOTS * TOK, HEAD).T
        slope = slope_ref[p * MINE + h] * LOG2E
        for slot in range(SLOTS):
            if slot < SPAN:
                count = times[x, z_before, slot + 1, 0:1, :] * has_before
                place = times[x, z_before, slot + 1, 1:2, :]
            else:
                count = times[x, z, slot - SPAN, 0:1, :]
                place = times[x, z, slot - SPAN, 1:2, :]
            shift = (place - base).astype(F32) * slope
            bias[slot] = jnp.where(token < count, shift, HIDDEN)
        dk_acc[h] = jnp.zeros((SLOTS, TOK, HEAD), F32)
        dv_acc[h] = jnp.zeros((SLOTS, TOK, HEAD), F32)
        wait(qb.at[h], in_recv.at[2, h])
        wait(gb.at[h], in_recv.at[3, h])

        def stretch(i):
            q = qb[h, i]
            live = token < times[x, z, i, 0:1, :]
            grad = jnp.where(live, gb[h, i].astype(F32), 0.0)
            go = (gate[h, pl.ds(i, 1), :] * grad).astype(BF16)
            top = jnp.full((1, TOK), HIDDEN, F32)
            for k in range(SPAN + 1):
                one = bias[i + k]
                value = dot(kb[h, i + k], q, NT) * (SCALE * LOG2E) + jnp.concatenate([one, one], axis=1)
                x_s[k] = value
                top = jnp.maximum(top, jnp.max(value, axis=0, keepdims=True))
            total = jnp.zeros((1, TOK), F32)
            for k in range(SPAN + 1):
                value = jnp.exp2(x_s[k] - top)
                x_s[k] = value
                total = total + jnp.sum(value, axis=0, keepdims=True)
            inverse = 1.0 / total
            for k in range(SPAN + 1):
                value = x_s[k] * inverse
                x_s[k] = value
                p_s[k] = value.astype(BF16)
            window = pl.ds(pl.multiple_of(i * TOK, TOK), (SPAN + 1) * TOK)
            out_t = dot(vt[:, window], p_s[...].reshape((SPAN + 1) * TOK, TOK))
            delta = jnp.sum(go.astype(F32).T * out_t, axis=0, keepdims=True)
            dgate[pl.ds(h * NY + i, 1), :] = jnp.sum(grad * out_t.T, axis=0, keepdims=True)
            for k in range(SPAN + 1):
                d_s[k] = (x_s[k] * (dot(vb[h, i + k], go, NT) - delta) * SCALE).astype(BF16)
            dq_s[h, i] = dot(kt[:, window], d_s[...].reshape((SPAN + 1) * TOK, TOK)).T.astype(BF16)
            for k in range(SPAN + 1):
                dk_acc[h, i + k] += dot(d_s[k], q)
                dv_acc[h, i + k] += dot(p_s[k], go)

        loop(0, NY, stretch)
        halo_s[h, 0] = dk_acc[h, 0:SPAN].astype(BF16)
        halo_s[h, 1] = dv_acc[h, 0:SPAN].astype(BF16)
        send(halo_s.at[h], halo_r.at[h], h_send.at[h], h_recv.at[h], z_dev(NZ - 1))

    def give_back(a, staged, out, h):
        def one(k):
            device, owner = group_dev(k)
            send(
                staged.at[h, owner // NS, pl.ds((owner % NS) * PART, PART)], out.at[:, column(p, h)],
                o_send.at[a], o_recv.at[a], device,
            )

        loop(1, GROUP, one)
        pltpu.make_async_copy(
            staged.at[h, y, pl.ds(s * PART, PART)], out.at[:, column(p, h)], o_loc.at[a]
        ).start()

    has_after = jnp.minimum(NZ - 1 - z, 1).astype(F32)

    def finish(h):
        wait(halo_r.at[h], h_recv.at[h])
        for n, (acc, staged) in enumerate(((dk_acc, dk_s), (dv_acc, dv_s))):
            staged[h, 0] = acc[h, SPAN].astype(BF16)
            for i in range(1, NY):
                staged[h, i] = (
                    acc[h, SPAN + i] + halo_r[h, n, i - 1].astype(F32) * has_after
                ).astype(BF16)
        give_back(1, dk_s, dk_out, h)
        give_back(2, dv_s, dv_out, h)

    dgate[...] = jnp.zeros_like(dgate)
    for h in range(MINE):
        head(h)
        give_back(0, dq_s, dq_out, h)
        if h > 0:
            finish(h - 1)

    terms[s, x, z, y] = dgate[...].astype(BF16)
    mine = terms.at[s, x, z, y]
    loop(1, NY, lambda k: send(mine, mine, t_send.at[0], t_recv.at[0], y_dev(k)))
    wait(terms.at[0, 0, 0, pl.ds(0, NY - 1)], t_recv.at[0])
    along_y = terms.at[s, x, z]
    loop(1, NZ, lambda k: send(along_y, along_y, t_send.at[1], t_recv.at[1], z_dev(k)))
    wait(terms.at[0, 0, pl.ds(0, NZ - 1)], t_recv.at[1])
    along_z = terms.at[s, x]
    loop(1, NX, lambda k: send(along_z, along_z, t_send.at[2], t_recv.at[2], x_dev(k)))
    finish(MINE - 1)
    wait(terms.at[0, pl.ds(0, NX - 1)], t_recv.at[2])
    along_x = terms.at[s]
    send(along_x, along_x, t_send.at[3], t_recv.at[3], (x, frame, 1 - s))
    wait(terms.at[0], t_recv.at[3])

    row = lax.broadcasted_iota(jnp.int32, (16, HEAD), 0)
    for h in range(MINE):
        keep = jnp.where(row // NY == h, 1.0, 0.0).astype(BF16)
        for other in range(NY):
            cores = [
                (terms[core, :, :, other] * keep).reshape(NX * NZ * 16, HEAD) for core in range(NS)
            ]
            both = jnp.concatenate(cores, axis=1)
            part = dot(emb_hi[...], both, TN) + dot(emb_lo[...], both, TN)
            for core in range(NS):
                at = (other * NS + core) * CHUNK + h * HEAD
                mod_out[:, at : at + HEAD] = part[:, core * HEAD : (core + 1) * HEAD]

    outs = (dq_out, dk_out, dv_out)
    arrived = pl.ds(0, (GROUP - 1) * CHUNK)
    for a in range(3):
        wait(outs[a].at[:, arrived], o_recv.at[a])
        wait(outs[a].at[:, arrived], o_send.at[a])
        wait(outs[a].at[:, pl.ds(0, CHUNK)], o_loc.at[a])
    for a in range(4):
        for h in range(MINE):
            wait(q_in.at[:, pl.ds(0, (GROUP - 1) * HEAD)], in_send.at[a, h])
    for h in range(MINE):
        wait(kb.at[h, pl.ds(0, SPAN)], z_send.at[0, h])
        wait(vb.at[h, pl.ds(0, SPAN)], z_send.at[1, h])
        wait(halo_s.at[h], h_send.at[h])
    wait(meta.at[pl.ds(0, NY - 1)], m_send.at[0])
    wait(times.at[0, pl.ds(0, NZ - 1)], m_send.at[1])
    wait(times.at[pl.ds(0, NX - 1)], m_send.at[2])
    wait(terms.at[0, 0, 0, pl.ds(0, NY - 1)], t_send.at[0])
    wait(terms.at[0, 0, pl.ds(0, NZ - 1)], t_send.at[1])
    wait(terms.at[0, pl.ds(0, NX - 1)], t_send.at[2])
    wait(terms.at[0], t_send.at[3])


def local(
    queries, key_states, value_states, out_grad, head_slopes, timesteps, stretch_frames,
    valid_counts, mod_weight,
):
    half = FREQ // 2
    freq = jnp.asarray(
        np.exp(-math.log(10000.0) * np.arange(half) / half).astype(np.float32)[None, :]
    )
    flat = (PART, WIDTH)
    anywhere = pl.BlockSpec(memory_space=pl.ANY)
    smem = pl.BlockSpec(memory_space=pltpu.SMEM)
    vmem = pl.BlockSpec(memory_space=pltpu.VMEM)
    dma = pltpu.SemaphoreType.DMA
    grad = jax.ShapeDtypeStruct(flat, BF16)
    dq, dk, dv, mod = pl.pallas_call(
        main_kernel,
        name="attention_backward",
        out_shape=(grad, grad, grad, jax.ShapeDtypeStruct((FREQ, WIDTH), F32)),
        in_specs=[vmem, smem, smem, smem, smem] + [anywhere] * 5,
        out_specs=(anywhere, anywhere, anywhere, vmem),
        scratch_shapes=[
            pltpu.VMEM((MINE, NY, TOK, HEAD), BF16),
            pltpu.VMEM((MINE, SLOTS, TOK, HEAD), BF16),
            pltpu.VMEM((MINE, SLOTS, TOK, HEAD), BF16),
            pltpu.VMEM((MINE, NY, TOK, HEAD), BF16),
            pltpu.VMEM((HEAD, SLOTS * TOK), BF16),
            pltpu.VMEM((HEAD, SLOTS * TOK), BF16),
            pltpu.VMEM((FREQ, CHUNK), F32),
            pltpu.VMEM((NY, 8, HEAD), jnp.int32),
            pltpu.VMEM((NX, NZ, NY, 8, HEAD), jnp.int32),
            pltpu.VMEM((NX * NZ * NY, HEAD), F32),
            pltpu.VMEM((MINE, 8, HEAD), F32),
            pltpu.VMEM((NX * NZ * 16, FREQ), BF16),
            pltpu.VMEM((NX * NZ * 16, FREQ), BF16),
            pltpu.VMEM((SLOTS, TOK, HEAD), F32),
            pltpu.VMEM((SPAN + 1, TOK, TOK), F32),
            pltpu.VMEM((SPAN + 1, TOK, TOK), BF16),
            pltpu.VMEM((SPAN + 1, TOK, TOK), BF16),
            pltpu.VMEM((MINE, SLOTS, TOK, HEAD), F32),
            pltpu.VMEM((MINE, SLOTS, TOK, HEAD), F32),
            pltpu.VMEM((MINE, NY, TOK, HEAD), BF16),
            pltpu.VMEM((MINE, NY, TOK, HEAD), BF16),
            pltpu.VMEM((MINE, NY, TOK, HEAD), BF16),
            pltpu.VMEM((MINE, 2, SPAN, TOK, HEAD), BF16),
            pltpu.VMEM((MINE, 2, SPAN, TOK, HEAD), BF16),
            pltpu.VMEM((16, HEAD), F32),
            pltpu.VMEM((NS, NX, NZ, NY, 16, HEAD), BF16),
            dma((4, MINE)), dma((4, MINE)),
            dma((2, MINE)), dma((2, MINE)),
            dma((MINE,)), dma((MINE,)),
            dma((3,)), dma((3,)), dma((3,)),
            dma((3,)), dma((3,)),
            dma((4,)), dma((4,)),
            dma,
        ],
        compiler_params=pltpu.CompilerParams(
            collective_id=0, has_side_effects=True, vmem_limit_bytes=48 * 2**20
        ),
    )(
        freq, head_slopes, timesteps.reshape(1), stretch_frames.reshape(1), valid_counts.reshape(1),
        mod_weight, queries.reshape(flat), key_states.reshape(flat), value_states.reshape(flat),
        out_grad.reshape(flat),
    )
    whole = (1, 1, PART, WIDTH)
    return dq.reshape(whole), dk.reshape(whole), dv.reshape(whole), mod


def solution(mesh):
    tokens = P("dp", "frame", "spatial", None)
    each = P("dp", "frame")
    return jax.shard_map(
        local,
        mesh=mesh,
        in_specs=(tokens, tokens, tokens, tokens, P(), each, each, each, P()),
        out_specs=(tokens, tokens, tokens, P()),
        check_vma=False,
    )
```

time: 971 us -> 103 us (0.11); the launches traced: 961 us -> 103 us
  blocking collectives: 754 us -> 0 us
  Pallas kernels: 0 us -> 90.1 us
  starting transfers between devices: 67.7 us -> 0 us
  matrix products: 45 us -> 0 us
  local copies, waits for them, and re-layouts: 37.7 us -> 10.1 us
  waiting for transfers between devices: 21.6 us -> 0 us
  other arithmetic: 18.3 us -> 0 us
  between operations: 16.3 us -> 2.6 us
    psum x1 -> x0, blocking collectives: 609 us -> none  [local(): lax.psum(embedding[:, None] * gate_grad[None, :], ('dp', 'frame'))]
    all_to_all x4 -> x0, blocking collectives: 145 us -> none  [the longest x1 124 us: local(): lax.all_to_all(query_grad, 'spatial', split_axis=0, concat_axis=1, tiled=...]
    pallas_call x0 -> x1, Pallas kernels: none -> 90.1 us  [local(): pl.pallas_call(main_kernel, name='attention_backward', out_shape=(grad, g...]
    ppermute x18 -> x0, starting transfers between devices: 53.7 us -> none  [shifted(): return lax.ppermute(block, axis, route)]
    dot_general x6 -> x0, matrix products: 36.3 us -> none  [the longest x1 9.42 us: local(): jnp.einsum('hij,ihe->jhe', attn_low, gated_grad, preferred_element_type=j...]
    ppermute x18 -> x0, waiting for transfers between devices: 21.6 us -> none  [shifted(): return lax.ppermute(block, axis, route)]
    all_to_all x3 -> x0, starting transfers between devices: 14 us -> none  [the longest x1 6.09 us: local(): lax.all_to_all(by_heads(queries), 'spatial', split_axis=1, concat_axis=0,...]
    convert_element_type x6 -> x0, other arithmetic: 11.7 us -> none  [the longest x1 3.43 us: local(): mod_weight_grad = lax.all_gather(weight_block.astype(jnp.bfloat16), 'spat...]
  transfers between devices with their start and end apart: 22 -> 0, of which waited for: 2 -> 0; matrix products, arithmetic and copies ran while one was open for 6% -> 0% of each run, Pallas kernels for 0% -> 0%
where the time goes in v1:
time: 103 us
  Pallas kernels  90.1 us (87%)
  local copies, waits for them, and re-layouts  10.1 us (10%)
  between operations  2.6 us (3%)
    pallas_call x1, Pallas kernels, local(): pl.pallas_call(main_kernel, name='attention_backward', out_shape=(grad, g...  90.1 us
    unnamed x18, local copies, waits for them, and re-layouts  10.1 us

profile of v1, /device:TPU:1, one launch (start us, length us, event | category | flops | bytes accessed | tf_op | source)
XLA Modules:
  0.0 102.9 jit_solution(7219516555810718323)
XLA Ops:
  2.6 0.0 copy-start
  2.6 1.1 %copy-done = bf16[1,1,128,3072]{3,2,1,0:T(8,128)(2,1)S(1)} copy-done((bf16[1,1,128,3072]{3,2,1,0:T(8,128)(2,1)S(1)}, bf16[1,1,128,3072]{3,2,1,0:T(8,128)(2,1)}, u32[]{:S(2)}) %copy-start) | copy-done | bytes 786456
  3.7 0.0 copy-start.1
  3.7 1.1 %copy-done.1 = bf16[1,1,128,3072]{3,2,1,0:T(8,128)(2,1)S(1)} copy-done((bf16[1,1,128,3072]{3,2,1,0:T(8,128)(2,1)S(1)}, bf16[1,1,128,3072]{3,2,1,0:T(8,128)(2,1)}, u32[]{:S(2)}) %copy-start.1) | copy-done | bytes 786456
  4.8 0.0 copy-start.2
  4.8 1.1 %copy-done.2 = bf16[1,1,128,3072]{3,2,1,0:T(8,128)(2,1)S(1)} copy-done((bf16[1,1,128,3072]{3,2,1,0:T(8,128)(2,1)S(1)}, bf16[1,1,128,3072]{3,2,1,0:T(8,128)(2,1)}, u32[]{:S(2)}) %copy-start.2) | copy-done | bytes 786456
  6.0 0.0 copy-start.3
  6.0 1.1 %copy-done.3 = bf16[1,1,128,3072]{3,2,1,0:T(8,128)(2,1)S(1)} copy-done((bf16[1,1,128,3072]{3,2,1,0:T(8,128)(2,1)S(1)}, bf16[1,1,128,3072]{3,2,1,0:T(8,128)(2,1)}, u32[]{:S(2)}) %copy-start.3) | copy-done | bytes 786456
  7.1 0.0 copy-start.4
  7.1 0.7 copy-done.4
  7.8 0.0 copy-start.5
  7.8 0.7 copy-done.5
  8.4 90.1 %attention_backward.1 = (bf16[128,3072]{1,0:T(8,128)(2,1)S(1)}, bf16[128,3072]{1,0:T(8,128)(2,1)S(1)}, bf16[128,3072]{1,0:T(8,128)(2,1)S(1)}, f32[256,3072]{1,0:T(8,128)}) custom-call(f32[1,128]{1,0:T(1,128)S(1)} %copy-done.5, f32[24]{0:T(128)S(1)} %copy-done.4, s32[1]{0:T(128)} %bitcast.10.step_ref, s32[1]{0:T(128)} %bitcast.11.frame_ref, ...), custom_call_target="tpu_custom_call" | custom-call | tf_op jit(solution)/shard_map/attention_backward/pallas_call | solution.py:346
  98.6 0.0 copy-start.6
  98.6 0.9 copy.21
  99.5 0.9 copy.22
  100.3 0.9 copy.23
  101.2 0.0 copy-done.6
  101.2 1.7 %copy.24 = f32[256,3072]{1,0:T(8,128)} copy(f32[256,3072]{1,0:T(8,128)S(1)} %copy-done.6) | data formatting | bytes 6291456
Async XLA Ops:
  2.6 1.1 %copy-start = (bf16[1,1,128,3072]{3,2,1,0:T(8,128)(2,1)S(1)}, bf16[1,1,128,3072]{3,2,1,0:T(8,128)(2,1)}, u32[]{:S(2)}) copy-start(bf16[1,1,128,3072]{3,2,1,0:T(8,128)(2,1)} %param.10) | copy-start | bytes 2359300
  3.7 1.1 %copy-start.1 = (bf16[1,1,128,3072]{3,2,1,0:T(8,128)(2,1)S(1)}, bf16[1,1,128,3072]{3,2,1,0:T(8,128)(2,1)}, u32[]{:S(2)}) copy-start(bf16[1,1,128,3072]{3,2,1,0:T(8,128)(2,1)} %param.11) | copy-start | bytes 2359300
  4.8 1.1 %copy-start.2 = (bf16[1,1,128,3072]{3,2,1,0:T(8,128)(2,1)S(1)}, bf16[1,1,128,3072]{3,2,1,0:T(8,128)(2,1)}, u32[]{:S(2)}) copy-start(bf16[1,1,128,3072]{3,2,1,0:T(8,128)(2,1)} %param.12) | copy-start | bytes 2359300
  6.0 1.1 %copy-start.3 = (bf16[1,1,128,3072]{3,2,1,0:T(8,128)(2,1)S(1)}, bf16[1,1,128,3072]{3,2,1,0:T(8,128)(2,1)}, u32[]{:S(2)}) copy-start(bf16[1,1,128,3072]{3,2,1,0:T(8,128)(2,1)} %param.13) | copy-start | bytes 2359300
  7.1 0.7 copy-start.4
  7.8 0.7 copy-start.5
  98.6 2.7 %copy-start.6 = (f32[256,3072]{1,0:T(8,128)S(1)}, f32[256,3072]{1,0:T(8,128)}, u32[]{:S(2)}) copy-start(f32[256,3072]{1,0:T(8,128)} %get-tuple-element.19) | copy-start | bytes 9437188

commit v2 on v1

--- a/solution.py
+++ b/solution.py
@@ -2,7 +2,6 @@
 
 import jax
 import jax.numpy as jnp
-import numpy as np
 from jax import lax
 from jax.experimental import pallas as pl
 from jax.experimental.pallas import tpu as pltpu
@@ -37,11 +36,11 @@
 
 
 def main_kernel(
-    freq_ref, slope_ref, step_ref, frame_ref, count_ref, weight_ref,
+    slope_ref, step_ref, frame_ref, count_ref, weight_ref,
     q_in, k_in, v_in, g_in,
     dq_out, dk_out, dv_out, mod_out,
-    qb, kb, vb, gb, kt, vt, weight, meta, times, rows_t, gate, emb_hi, emb_lo, bias,
-    x_s, p_s, d_s, dk_acc, dv_acc, dq_s, dk_s, dv_s, halo_s, halo_r, dgate, terms,
+    qb, kb, vb, gb, kt, vt, weight, meta, times, rows_t, gate, emb, emb_hi, emb_lo, bias,
+    x_s, p_s, d_s, dk_acc, dv_acc, dq_s, dk_s, dv_s, halo_s, halo_r, dgate, rows_y, terms,
     in_recv, in_send, z_recv, z_send, h_recv, h_send, o_recv, o_send, o_loc,
     m_recv, m_send, t_recv, t_send, w_sem,
 ):
@@ -95,8 +94,10 @@
     )
     weight_copy.start()
     line = lax.broadcasted_iota(jnp.int32, (8, HEAD), 0)
+    steps = lax.broadcasted_iota(jnp.int32, (1, HEAD), 1).astype(F32)
+    freq = jnp.exp(steps * (-math.log(10000.0) / (FREQ // 2)))
     meta[y] = jnp.where(
-        line == 0, count_ref[0], jnp.where(line == 1, frame_ref[0], step_ref[0])
+        line == 0, count_ref[0, 0], jnp.where(line == 1, frame_ref[0, 0], step_ref[0, 0])
     )
     arrays = ((k_in, kb, SPAN), (v_in, vb, SPAN), (q_in, qb, 0), (g_in, gb, 0))
 
@@ -128,8 +129,9 @@
         for a in (first, first + 1):
             loop(1, GROUP, lambda k, a=a: send_part(a, h, k))
 
-    loop(0, MINE, lambda h: send_pair(0, h))
-    loop(0, MINE, lambda h: send_pair(2, h))
+    send_pair(0, 0)
+    send_pair(2, 0)
+    send_pair(0, 1)
 
     wait(meta.at[pl.ds(0, NY - 1)], m_recv.at[0])
     times[x, z] = meta[...]
@@ -137,11 +139,11 @@
     rows_t[...] = jnp.zeros_like(rows_t)
     for i in range(NY):
         rows_t[i : i + 1, :] = meta[i, 2:3, :].astype(F32)
-    angles = rows_t[0:8, :] * freq_ref[...]
-    emb = jnp.concatenate([jnp.cos(angles), jnp.sin(angles)], axis=1)
+    angles = rows_t[0:8, :] * freq
+    own_emb = jnp.concatenate([jnp.cos(angles), jnp.sin(angles)], axis=1)
     weight_copy.wait()
     gates = lax.dot_general(
-        emb, weight[...], (((1,), (0,)), ((), ())), precision=HIGHEST, preferred_element_type=F32
+        own_emb, weight[...], (((1,), (0,)), ((), ())), precision=HIGHEST, preferred_element_type=F32
     )
     for h in range(MINE):
         gate[h] = gates[:, h * HEAD : (h + 1) * HEAD]
@@ -158,10 +160,18 @@
             z_send.at[1, h], z_recv.at[1, h], z_dev(1),
         )
 
-    loop(0, 1, pass_on)
+    def arrive(h):
+        wait(qb.at[h], in_recv.at[2, h])
+        wait(gb.at[h], in_recv.at[3, h])
+
+    pass_on(0)
+    send_pair(0, 2)
     wait(times.at[0, pl.ds(0, NZ - 1)], m_recv.at[1])
     loop(1, NX, lambda k: send(times.at[x], times.at[x], m_send.at[2], m_recv.at[2], x_dev(k)))
-    loop(1, MINE, pass_on)
+    arrive(0)
+    send_pair(2, 1)
+    pass_on(1)
+    send_pair(2, 2)
 
     wait(times.at[pl.ds(0, NX - 1)], m_recv.at[2])
 
@@ -172,17 +182,17 @@
     loop(0, NX * NZ, take_row)
 
     def features(n):
-        angle = rows_t[pl.ds(pl.multiple_of(n * 8, 8), 8), :] * freq_ref[...]
+        angle = rows_t[pl.ds(pl.multiple_of(n * 8, 8), 8), :] * freq
         both = jnp.concatenate([jnp.cos(angle), jnp.sin(angle)], axis=1)
         for half in range(2):
             four = both[half * NY : (half + 1) * NY]
             tile = jnp.concatenate([four, four, four, four], axis=0)
-            high = tile.astype(BF16)
-            at = pl.ds(pl.multiple_of(n * 32 + half * 16, 16), 16)
-            emb_hi[at, :] = high
-            emb_lo[at, :] = (tile - high.astype(F32)).astype(BF16)
+            emb[pl.ds(pl.multiple_of(n * 32 + half * 16, 16), 16), :] = tile
 
     loop(0, NX * NZ // 2, features)
+    turned = emb[...].T
+    emb_hi[...] = turned.astype(BF16)
+    emb_lo[...] = (turned - turned.astype(BF16).astype(F32)).astype(BF16)
 
     token = lax.broadcasted_iota(jnp.int32, (TOK, HEAD), 0)
     z_before = (z + NZ - 1) % NZ
@@ -206,8 +216,6 @@
             bias[slot] = jnp.where(token < count, shift, HIDDEN)
         dk_acc[h] = jnp.zeros((SLOTS, TOK, HEAD), F32)
         dv_acc[h] = jnp.zeros((SLOTS, TOK, HEAD), F32)
-        wait(qb.at[h], in_recv.at[2, h])
-        wait(gb.at[h], in_recv.at[3, h])
 
         def stretch(i):
             q = qb[h, i]
@@ -233,7 +241,7 @@
             window = pl.ds(pl.multiple_of(i * TOK, TOK), (SPAN + 1) * TOK)
             out_t = dot(vt[:, window], p_s[...].reshape((SPAN + 1) * TOK, TOK))
             delta = jnp.sum(go.astype(F32).T * out_t, axis=0, keepdims=True)
-            dgate[pl.ds(h * NY + i, 1), :] = jnp.sum(grad * out_t.T, axis=0, keepdims=True)
+            dgate[h, pl.ds(y * NY + i, 1), :] = jnp.sum(grad * out_t.T, axis=0, keepdims=True)
             for k in range(SPAN + 1):
                 d_s[k] = (x_s[k] * (dot(vb[h, i + k], go, NT) - delta) * SCALE).astype(BF16)
             dq_s[h, i] = dot(kt[:, window], d_s[...].reshape((SPAN + 1) * TOK, TOK)).T.astype(BF16)
@@ -241,10 +249,11 @@
                 dk_acc[h, i + k] += dot(d_s[k], q)
                 dv_acc[h, i + k] += dot(p_s[k], go)
 
-        loop(0, NY, stretch)
+        loop(0, SPAN, stretch)
         halo_s[h, 0] = dk_acc[h, 0:SPAN].astype(BF16)
         halo_s[h, 1] = dv_acc[h, 0:SPAN].astype(BF16)
         send(halo_s.at[h], halo_r.at[h], h_send.at[h], h_recv.at[h], z_dev(NZ - 1))
+        stretch(SPAN)
 
     def give_back(a, staged, out, h):
         def one(k):
@@ -273,39 +282,66 @@
         give_back(2, dv_s, dv_out, h)
 
     dgate[...] = jnp.zeros_like(dgate)
-    for h in range(MINE):
-        head(h)
-        give_back(0, dq_s, dq_out, h)
-        if h > 0:
-            finish(h - 1)
-
-    terms[s, x, z, y] = dgate[...].astype(BF16)
-    mine = terms.at[s, x, z, y]
-    loop(1, NY, lambda k: send(mine, mine, t_send.at[0], t_recv.at[0], y_dev(k)))
-    wait(terms.at[0, 0, 0, pl.ds(0, NY - 1)], t_recv.at[0])
-    along_y = terms.at[s, x, z]
-    loop(1, NZ, lambda k: send(along_y, along_y, t_send.at[1], t_recv.at[1], z_dev(k)))
-    wait(terms.at[0, 0, pl.ds(0, NZ - 1)], t_recv.at[1])
-    along_z = terms.at[s, x]
-    loop(1, NX, lambda k: send(along_z, along_z, t_send.at[2], t_recv.at[2], x_dev(k)))
-    finish(MINE - 1)
-    wait(terms.at[0, pl.ds(0, NX - 1)], t_recv.at[2])
-    along_x = terms.at[s]
-    send(along_x, along_x, t_send.at[3], t_recv.at[3], (x, frame, 1 - s))
-    wait(terms.at[0], t_recv.at[3])
+    def along_y(h):
+        rows_y[h, y] = dgate[h].astype(BF16)
+        mine = rows_y.at[h, y]
+        loop(1, NY, lambda k: send(mine, mine, t_send.at[0, h], t_recv.at[0, h], y_dev(k)))
+
+    def along_z(h):
+        wait(rows_y.at[h, pl.ds(0, NY - 1)], t_recv.at[0, h])
+        terms[h, s, x, z] = jnp.sum(rows_y[h].astype(F32), axis=0).astype(BF16)
+        mine = terms.at[h, s, x, z]
+        loop(1, NZ, lambda k: send(mine, mine, t_send.at[1, h], t_recv.at[1, h], z_dev(k)))
+
+    def along_x(h):
+        wait(terms.at[h, 0, 0, pl.ds(0, NZ - 1)], t_recv.at[1, h])
+        mine = terms.at[h, s, x]
+        loop(1, NX, lambda k: send(mine, mine, t_send.at[2, h], t_recv.at[2, h], x_dev(k)))
+
+    def to_core(h):
+        wait(terms.at[h, 0, pl.ds(0, NX - 1)], t_recv.at[2, h])
+        send(terms.at[h, s], terms.at[h, s], t_send.at[3, h], t_recv.at[3, h], (x, frame, 1 - s))
 
     row = lax.broadcasted_iota(jnp.int32, (16, HEAD), 0)
-    for h in range(MINE):
-        keep = jnp.where(row // NY == h, 1.0, 0.0).astype(BF16)
+
+    def contract(h):
+        wait(terms.at[h, 0], t_recv.at[3, h])
         for other in range(NY):
-            cores = [
-                (terms[core, :, :, other] * keep).reshape(NX * NZ * 16, HEAD) for core in range(NS)
-            ]
+            keep = jnp.where(row // NY == other, 1.0, 0.0).astype(BF16)
+            cores = [(terms[h, core] * keep).reshape(NX * NZ * 16, HEAD) for core in range(NS)]
             both = jnp.concatenate(cores, axis=1)
-            part = dot(emb_hi[...], both, TN) + dot(emb_lo[...], both, TN)
+            part = dot(emb_hi[...], both) + dot(emb_lo[...], both)
             for core in range(NS):
                 at = (other * NS + core) * CHUNK + h * HEAD
                 mod_out[:, at : at + HEAD] = part[:, core * HEAD : (core + 1) * HEAD]
+
+    head(0)
+    along_y(0)
+    give_back(0, dq_s, dq_out, 0)
+    pass_on(2)
+    arrive(1)
+    head(1)
+    along_y(1)
+    give_back(0, dq_s, dq_out, 1)
+    arrive(2)
+    head(2)
+    along_y(2)
+    along_z(0)
+    give_back(0, dq_s, dq_out, 2)
+    finish(0)
+    finish(1)
+    along_z(1)
+    along_x(0)
+    along_z(2)
+    along_x(1)
+    to_core(0)
+    finish(2)
+    along_x(2)
+    to_core(1)
+    contract(0)
+    to_core(2)
+    contract(1)
+    contract(2)
 
     outs = (dq_out, dk_out, dv_out)
     arrived = pl.ds(0, (GROUP - 1) * CHUNK)
@@ -323,32 +359,33 @@
     wait(meta.at[pl.ds(0, NY - 1)], m_send.at[0])
     wait(times.at[0, pl.ds(0, NZ - 1)], m_send.at[1])
     wait(times.at[pl.ds(0, NX - 1)], m_send.at[2])
-    wait(terms.at[0, 0, 0, pl.ds(0, NY - 1)], t_send.at[0])
-    wait(terms.at[0, 0, pl.ds(0, NZ - 1)], t_send.at[1])
-    wait(terms.at[0, pl.ds(0, NX - 1)], t_send.at[2])
-    wait(terms.at[0], t_send.at[3])
+    for h in range(MINE):
+        wait(rows_y.at[h, pl.ds(0, NY - 1)], t_send.at[0, h])
+        wait(terms.at[h, 0, 0, pl.ds(0, NZ - 1)], t_send.at[1, h])
+        wait(terms.at[h, 0, pl.ds(0, NX - 1)], t_send.at[2, h])
+        wait(terms.at[h, 0], t_send.at[3, h])
+
+
+def in_hbm(array):
+    return pltpu.with_memory_space_constraint(array, pltpu.HBM)
 
 
 def local(
     queries, key_states, value_states, out_grad, head_slopes, timesteps, stretch_frames,
     valid_counts, mod_weight,
 ):
-    half = FREQ // 2
-    freq = jnp.asarray(
-        np.exp(-math.log(10000.0) * np.arange(half) / half).astype(np.float32)[None, :]
-    )
     flat = (PART, WIDTH)
     anywhere = pl.BlockSpec(memory_space=pl.ANY)
     smem = pl.BlockSpec(memory_space=pltpu.SMEM)
-    vmem = pl.BlockSpec(memory_space=pltpu.VMEM)
+    hbm = pl.BlockSpec(memory_space=pltpu.HBM)
     dma = pltpu.SemaphoreType.DMA
     grad = jax.ShapeDtypeStruct(flat, BF16)
     dq, dk, dv, mod = pl.pallas_call(
         main_kernel,
         name="attention_backward",
-        out_shape=(grad, grad, grad, jax.ShapeDtypeStruct((FREQ, WIDTH), F32)),
-        in_specs=[vmem, smem, smem, smem, smem] + [anywhere] * 5,
-        out_specs=(anywhere, anywhere, anywhere, vmem),
+        out_shape=(pltpu.VMEM(flat, BF16),) * 3 + (pltpu.VMEM((FREQ, WIDTH), F32),),
+        in_specs=[smem] * 4 + [hbm] * 5,
+        out_specs=(anywhere,) * 3 + (pl.BlockSpec(memory_space=pltpu.VMEM),),
         scratch_shapes=[
             pltpu.VMEM((MINE, NY, TOK, HEAD), BF16),
             pltpu.VMEM((MINE, SLOTS, TOK, HEAD), BF16),
@@ -361,8 +398,9 @@
             pltpu.VMEM((NX, NZ, NY, 8, HEAD), jnp.int32),
             pltpu.VMEM((NX * NZ * NY, HEAD), F32),
             pltpu.VMEM((MINE, 8, HEAD), F32),
-            pltpu.VMEM((NX * NZ * 16, FREQ), BF16),
-            pltpu.VMEM((NX * NZ * 16, FREQ), BF16),
+            pltpu.VMEM((NX * NZ * 16, FREQ), F32),
+            pltpu.VMEM((FREQ, NX * NZ * 16), BF16),
+            pltpu.VMEM((FREQ, NX * NZ * 16), BF16),
             pltpu.VMEM((SLOTS, TOK, HEAD), F32),
             pltpu.VMEM((SPAN + 1, TOK, TOK), F32),
             pltpu.VMEM((SPAN + 1, TOK, TOK), BF16),
@@ -374,23 +412,25 @@
             pltpu.VMEM((MINE, NY, TOK, HEAD), BF16),
             pltpu.VMEM((MINE, 2, SPAN, TOK, HEAD), BF16),
             pltpu.VMEM((MINE, 2, SPAN, TOK, HEAD), BF16),
-            pltpu.VMEM((16, HEAD), F32),
-            pltpu.VMEM((NS, NX, NZ, NY, 16, HEAD), BF16),
+            pltpu.VMEM((MINE, 16, HEAD), F32),
+            pltpu.VMEM((MINE, NY, 16, HEAD), BF16),
+            pltpu.VMEM((MINE, NS, NX, NZ, 16, HEAD), BF16),
             dma((4, MINE)), dma((4, MINE)),
             dma((2, MINE)), dma((2, MINE)),
             dma((MINE,)), dma((MINE,)),
             dma((3,)), dma((3,)), dma((3,)),
             dma((3,)), dma((3,)),
-            dma((4,)), dma((4,)),
+            dma((4, MINE)), dma((4, MINE)),
             dma,
         ],
         compiler_params=pltpu.CompilerParams(
             collective_id=0, has_side_effects=True, vmem_limit_bytes=48 * 2**20
         ),
     )(
-        freq, head_slopes, timesteps.reshape(1), stretch_frames.reshape(1), valid_counts.reshape(1),
-        mod_weight, queries.reshape(flat), key_states.reshape(flat), value_states.reshape(flat),
-        out_grad.reshape(flat),
+        in_hbm(head_slopes), timesteps, stretch_frames,
+        valid_counts, in_hbm(mod_weight), in_hbm(queries.reshape(flat)),
+        in_hbm(key_states.reshape(flat)), in_hbm(value_states.reshape(flat)),
+        in_hbm(out_grad.reshape(flat)),
     )
     whole = (1, 1, PART, WIDTH)
     return dq.reshape(whole), dk.reshape(whole), dv.reshape(whole), mod

time: 103 us -> 87.8 us (0.85)
  Pallas kernels: 90.1 us -> 80.8 us
  local copies, waits for them, and re-layouts: 10.1 us -> 4.3 us
    pallas_call x1, Pallas kernels: 90.1 us -> 80.8 us  [local(): pl.pallas_call(main_kernel, name='attention_backward', out_shape=(pltpu.V...]
    unnamed x18 -> x4, local copies, waits for them, and re-layouts: 10.1 us -> 4.3 us
where the time goes in v2:
time: 87.8 us; the launch traced here: 87.7 us
  Pallas kernels  80.8 us (92%)
  local copies, waits for them, and re-layouts  4.3 us (5%)
  between operations  2.58 us (3%)
    pallas_call x1, Pallas kernels, local(): pl.pallas_call(main_kernel, name='attention_backward', out_shape=(pltpu.V...  80.8 us
    unnamed x4, local copies, waits for them, and re-layouts  4.3 us

profile of v2, /device:TPU:1, one launch (start us, length us, event | category | flops | bytes accessed | tf_op | source)
XLA Modules:
  0.0 87.7 jit_solution(6362328918790548773)
XLA Ops:
  2.6 80.8 %attention_backward.1 = (bf16[128,3072]{1,0:T(8,128)(2,1)S(1)}, bf16[128,3072]{1,0:T(8,128)(2,1)S(1)}, bf16[128,3072]{1,0:T(8,128)(2,1)S(1)}, f32[256,3072]{1,0:T(8,128)S(1)}) custom-call(f32[24]{0:T(128)} %slope_ref.1, s32[1,1]{1,0:T(1,128)S(6)} %copy.21.step_ref, s32[1,1]{1,0:T(1,128)S(6)} %copy.22.frame_ref, s32[1,1]{1,0:T(1,128)S(6)} %copy.23.count_ref, ...), custom_call_target="tpu_custom_call" | custom-call | tf_op jit(solution)/shard_map/attention_backward/pallas_call | solution.py:383
  83.4 0.9 %copy.17 = bf16[1,1,128,3072]{3,2,1,0:T(8,128)(2,1)} copy(bf16[1,1,128,3072]{3,2,1,0:T(8,128)(2,1)S(1)} %bitcast.9) | data formatting | bytes 1572864
  84.3 0.9 %copy.18 = bf16[1,1,128,3072]{3,2,1,0:T(8,128)(2,1)} copy(bf16[1,1,128,3072]{3,2,1,0:T(8,128)(2,1)S(1)} %bitcast.8) | data formatting | bytes 1572864
  85.1 0.9 %copy.19 = bf16[1,1,128,3072]{3,2,1,0:T(8,128)(2,1)} copy(bf16[1,1,128,3072]{3,2,1,0:T(8,128)(2,1)S(1)} %bitcast.7) | data formatting | bytes 1572864
  86.0 1.7 %copy.20 = f32[256,3072]{1,0:T(8,128)} copy(f32[256,3072]{1,0:T(8,128)S(1)} %get-tuple-element.15) | data formatting | bytes 6291456
